TPU v7x, 32 devices: a whole 2x2x4 slice. The times are simulated.
32 devices in a mesh: row: 4 (over y, x), col: 8 (over z, core).
Axes of the slice: x: 2, y: 2, z: 4, core: 2. Of those that a mesh axis runs over, the one named last changes fastest.
Arguments:
- z_slab: float32 [1024, 1024], P('col', 'row'), may hold values from -6 to 6
- prev_factor: bfloat16 [1024, 32768], P('row', 'col'), may hold values from -0.03125 to 0.03125
- prev_solution: bfloat16 [1024, 32768], P(None, 'col'), may hold values from -6 to 6
- slab_factor: bfloat16 [1024, 1024], P('row'), may hold values from -0.09375 to 0.09375
- diag_inverse: bfloat16 [1024, 256], P('row'), may hold values from -1 to 2, as said below
Outputs:
- solved: float32 [1024, 1024], P('col', 'row')
Inputs may be any that keep to these rules, and one draw needn't show every extreme that they name: `diag_inverse`: each 256 x 256 block is lower triangular with its diagonal between 1 and 2.
All inputs are finite; a program needn't handle non-finite values.
Results may differ from a plain program's by a relative error of at most 0.0003.
Values sent between devices are 32-bit elements; how exact they have to be, the bound alone decides.
A program may use at most 64 MiB of HBM per device.

v0:
```python
import jax
import jax.numpy as jnp
from jax import lax
from jax.sharding import PartitionSpec as P


def spread(block, axis, owner):
    block = jnp.where(lax.axis_index(axis) == owner, block, jnp.zeros_like(block))
    return lax.psum(block, axis)


def precise_dot(left, right):
    return lax.dot_general(
        left,
        right,
        (((1,), (1,)), ((), ())),
        precision=lax.Precision.HIGHEST,
        preferred_element_type=jnp.float32,
    )


def on_device(z_slab, prev_factor, prev_solution, slab_factor, diag_inverse):
    row_count = z_slab.shape[0]
    block_width = diag_inverse.shape[1]
    block_rows = lax.axis_size("row")
    partial_value = lax.dot_general(
        prev_solution, prev_factor, (((1,), (1,)), ((), ())), preferred_element_type=jnp.float32
    )
    summed = lax.psum(partial_value, "col")
    fan_sum = lax.dynamic_slice_in_dim(summed, lax.axis_index("col") * row_count, row_count, 0)
    remainder = z_slab - fan_sum
    factor = slab_factor.astype(jnp.float32)
    inverse = diag_inverse.astype(jnp.float32)
    device_row = lax.axis_index("row")
    result = jnp.zeros((row_count, block_width), jnp.float32)
    updates = jnp.zeros((row_count, block_width), jnp.float32)

    def bcast_step(block_index, carry):
        result, updates = carry
        candidate = precise_dot(remainder - updates, inverse)
        arrived = spread(candidate, "row", block_index)
        result = jnp.where(device_row == block_index, arrived, result)
        columns = lax.dynamic_slice_in_dim(factor, block_index * block_width, block_width, 1)
        updates = updates + precise_dot(arrived, columns)
        return (result, updates)

    result, updates = lax.fori_loop(0, block_rows, bcast_step, (result, updates))
    return result


def solution(mesh):
    in_specs = (P("col", "row"), P("row", "col"), P(None, "col"), P("row", None), P("row", None))
    out_specs = P("col", "row")
    return jax.shard_map(
        on_device, mesh=mesh, in_specs=in_specs, out_specs=out_specs, check_vma=False
    )
```

profile of v0, /device:TPU:0, one launch (start us, length us, event | category | flops | bytes accessed | tf_op | source)
XLA Modules:
  0.0 277.1 jit_solution(165684188814202454)
XLA Ops:
  6.5 0.0 copy-start
  6.5 0.0 all-reduce.3.cloned.1.call-start
  6.5 1.6 copy-done
  8.1 6.8 %fusion.7 = f32[1024,256]{1,0:T(8,128)} fusion(bf16[1024,4096]{1,0:T(8,128)(2,1)} %param.9, bf16[256,4096]{1,0:T(8,128)(2,1)S(1)} %copy-done), kind=kOutput, calls=%fused_computation.11 | convolution fusion | flops 2147483648 | bytes 11534336 | tf_op jit(solution)/shard_map/dot_general | solution.py:26
  14.9 0.0 all-reduce.3.cloned.1.call-update
  14.9 1.1 convert_element_type.7
  16.1 0.9 convert_element_type.6
  17.0 59.6 %all-reduce.3.cloned.1.call-done = f32[1024,256]{1,0:T(8,128)} async-done(((f32[1024,256]{1,0:T(8,128)}), f32[1024,256]{1,0:T(8,128)}) %all-reduce.3.cloned.1.call-update) | async-done | bytes 1048592 | tf_op jit(solution)/shard_map/psum | solution.py:29
  76.6 1.6 dynamic-slice_subtract_fusion
  78.3 192.3 %while.16 = (s32[]{:T(128)}, f32[128,256]{1,0:T(8,128)}, f32[128,256]{1,0:T(8,128)S(1)}, s32[]{:T(128)}, f32[128,256]{1,0:T(8,128)}, /*index=5*/f32[256,256]{1,0...) while((s32[]{:T(128)}, f32[128,256]{1,0:T(8,128)}, ...), condition=%wide.region_3.4_spmd.clone, body=%wide.region_1.3_spmd.clone.sunk | while | flops 201588736 | bytes 2490639 | solution.py:47
  78.3 0.0 all-reduce.5.cloned.1.call-start
  78.3 1.9 convolution_select_fusion.2
  80.2 0.0 all-reduce.5.cloned.1.call-update
  80.3 42.7 %all-reduce.5.cloned.1.call-done = f32[128,256]{1,0:T(8,128)} async-done(((f32[128,256]{1,0:T(8,128)}), f32[128,256]{1,0:T(8,128)}) %all-reduce.5.cloned.1.call-update) | async-done | bytes 131088 | tf_op jit(solution)/shard_map/while/body/eval_jaxpr/psum | solution.py:9
  123.0 1.4 convolution_add_fusion.2
  124.3 1.6 select_select_fusion.2
  125.9 2.0 convolution_select_fusion.2
  127.9 0.0 all-reduce.5.cloned.1.call-update
  127.9 42.9 %all-reduce.5.cloned.1.call-done = f32[128,256]{1,0:T(8,128)} async-done(((f32[128,256]{1,0:T(8,128)}), f32[128,256]{1,0:T(8,128)}) %all-reduce.5.cloned.1.call-update) | async-done | bytes 131088 | tf_op jit(solution)/shard_map/while/body/eval_jaxpr/psum | solution.py:9
  170.8 1.4 convolution_add_fusion.2
  172.1 1.6 select_select_fusion.2
  173.7 0.0 all-reduce.5.cloned.1.call-start
  173.7 1.9 convolution_select_fusion.2
  175.7 0.0 all-reduce.5.cloned.1.call-update
  175.7 43.5 %all-reduce.5.cloned.1.call-done = f32[128,256]{1,0:T(8,128)} async-done(((f32[128,256]{1,0:T(8,128)}), f32[128,256]{1,0:T(8,128)}) %all-reduce.5.cloned.1.call-update) | async-done | bytes 131088 | tf_op jit(solution)/shard_map/while/body/eval_jaxpr/psum | solution.py:9
  219.2 1.4 convolution_add_fusion.2
  220.6 1.6 select_select_fusion.2
  222.2 1.9 convolution_select_fusion.2
  224.1 0.0 all-reduce.5.cloned.1.call-update
  224.2 43.4 %all-reduce.5.cloned.1.call-done = f32[128,256]{1,0:T(8,128)} async-done(((f32[128,256]{1,0:T(8,128)}), f32[128,256]{1,0:T(8,128)}) %all-reduce.5.cloned.1.call-update) | async-done | bytes 131088 | tf_op jit(solution)/shard_map/while/body/eval_jaxpr/psum | solution.py:9
  267.6 1.4 convolution_add_fusion.2
  269.0 1.6 select_select_fusion.2
  (4 shorter events, 0.0 us)
Async XLA Ops:
  6.5 1.6 copy-start
  6.5 70.1 %all-reduce.3.cloned.1.call-start = ((), (), s32[]{:S(2)}) async-start(), calls=%async_computation | async-start | bytes 2097152 | tf_op jit(solution)/shard_map/psum | solution.py:29
  78.3 44.7 %all-reduce.5.cloned.1.call-start = ((), (), s32[]{:S(2)}) async-start(), calls=%async_computation.1 | async-start | bytes 262144 | tf_op jit(solution)/shard_map/while/body/eval_jaxpr/psum | solution.py:9
  125.9 44.9 %all-reduce.5.cloned.1.call-start = ((), (), s32[]{:S(2)}) async-start(), calls=%async_computation.1 | async-start | bytes 262144 | tf_op jit(solution)/shard_map/while/body/eval_jaxpr/psum | solution.py:9
  173.7 45.5 %all-reduce.5.cloned.1.call-start = ((), (), s32[]{:S(2)}) async-start(), calls=%async_computation.1 | async-start | bytes 262144 | tf_op jit(solution)/shard_map/while/body/eval_jaxpr/psum | solution.py:9
  222.2 45.4 %all-reduce.5.cloned.1.call-start = ((), (), s32[]{:S(2)}) async-start(), calls=%async_computation.1 | async-start | bytes 262144 | tf_op jit(solution)/shard_map/while/body/eval_jaxpr/psum | solution.py:9
Sparse Core Ops, SparseCore 0:
  15.0 61.5 all-reduce.2
  82.0 40.9 all-reduce.4
  129.6 41.1 all-reduce.4
  177.1 42.0 all-reduce.4
  225.6 41.9 all-reduce.4
where the time goes:
time: 278 us; the launch traced here: 277 us
  waiting for transfers between devices  232 us (83%)
  matrix products  20 us (7%)
  between operations  13.1 us (5%)
  other arithmetic  10.1 us (4%)
    psum x4, waiting for transfers between devices, spread(): return lax.psum(block, axis)  173 us
    psum x1, waiting for transfers between devices, on_device(): summed = lax.psum(partial_value, 'col')  59.6 us
    dot_general x8, matrix products, precise_dot(): lax.dot_general(left, right, (((1,), (1,)), ((), ())), precision=lax.Prec...  13.2 us
    dot_general x1, matrix products, on_device(): lax.dot_general(prev_solution, prev_factor, (((1,), (1,)), ((), ())), pre...  6.76 us
    select_n x4, other arithmetic, bcast_step(): result = jnp.where(device_row == block_index, arrived, result)  6.36 us
  transfers between devices with their start and end apart: 5, of which 5 were waited for; matrix products, arithmetic and copies ran while one was open for 1% of the time, Pallas kernels for 0%

commit v1 on v0

--- a/solution.py
+++ b/solution.py
@@ -26,7 +26,9 @@
     partial_value = lax.dot_general(
         prev_solution, prev_factor, (((1,), (1,)), ((), ())), preferred_element_type=jnp.float32
     )
-    summed = lax.psum(partial_value, "col")
+    summed = partial_value
+    for hop in (1, 2, 4):
+        summed = summed + lax.ppermute(summed, "col", [(dev, dev ^ hop) for dev in range(8)])
     fan_sum = lax.dynamic_slice_in_dim(summed, lax.axis_index("col") * row_count, row_count, 0)
     remainder = z_slab - fan_sum
     factor = slab_factor.astype(jnp.float32)

time: 278 us -> 296 us (1.065)
  waiting for transfers between devices: 232 us -> 244 us
  starting transfers between devices: 0.01 us -> 6.3 us
    ppermute x0 -> x3, waiting for transfers between devices: none -> 69.3 us  [on_device(): lax.ppermute(summed, 'col', [(dev, dev ^ hop) for dev in range(8)])]
    psum x1 -> x0, waiting for transfers between devices: 59.6 us -> none  [on_device(): summed = lax.psum(partial_value, 'col')]
    ppermute x0 -> x3, starting transfers between devices: none -> 6.29 us  [on_device(): lax.ppermute(summed, 'col', [(dev, dev ^ hop) for dev in range(8)])]
  transfers between devices with their start and end apart: 5 -> 7, of which waited for: 5 -> 7; matrix products, arithmetic and copies ran while one was open for 1% -> 1% of each run, Pallas kernels for 0% -> 0%
where the time goes in v1:
time: 296 us
  waiting for transfers between devices  244 us (82%)
  matrix products  19 us (6%)
  between operations  13.1 us (4%)
  other arithmetic  11.4 us (4%)
  starting transfers between devices  6.3 us (2%)
    psum x4, waiting for transfers between devices, spread(): return lax.psum(block, axis)  175 us
    ppermute x3, waiting for transfers between devices, on_device(): lax.ppermute(summed, 'col', [(dev, dev ^ hop) for dev in range(8)])  69.3 us
    dot_general x8, matrix products, precise_dot(): lax.dot_general(left, right, (((1,), (1,)), ((), ())), precision=lax.Prec...  13.2 us
    select_n x4, other arithmetic, bcast_step(): result = jnp.where(device_row == block_index, arrived, result)  6.36 us
    ppermute x3, starting transfers between devices, on_device(): lax.ppermute(summed, 'col', [(dev, dev ^ hop) for dev in range(8)])  6.29 us
  transfers between devices with their start and end apart: 7, of which 7 were waited for; matrix products, arithmetic and copies ran while one was open for 1% of the time, Pallas kernels for 0%

profile of v1, /device:TPU:0, one launch (start us, length us, event | category | flops | bytes accessed | tf_op | source)
XLA Modules:
  0.0 295.7 jit_solution(5577902164604195173)
XLA Ops:
  6.5 1.6 copy-done
  8.1 5.7 %fusion.8 = f32[1024,256]{1,0:T(8,128)S(1)} fusion(bf16[1024,4096]{1,0:T(8,128)(2,1)} %param.9, bf16[256,4096]{1,0:T(8,128)(2,1)S(1)} %copy-done), kind=kOutput, calls=%fused_computation.12 | convolution fusion | flops 2147483648 | bytes 11534336 | tf_op jit(solution)/shard_map/dot_general | solution.py:26
  13.9 0.5 collective-permute-start
  14.4 2.3 collective-permute-done
  16.7 0.1 add.44
  16.8 3.0 %collective-permute-start.1 = (f32[1024,256]{1,0:T(8,128)S(1)}, f32[1024,256]{1,0:T(8,128)S(1)}, u32[]{:S(2)}, u32[]{:S(2)}) collective-permute-start(f32[1024,256]{1,0:T(8,128)S(1)} %add.44), channel_id=1, source_target_pairs={{0,2},{1,3},{2,0},{3,1},{4,6},{5,7},{6,4},{7,5},{8,10},{9,11},{10,... | collective-permute-start | bytes 3145736 | tf_op jit(solution)/shard_map/ppermute | solution.py:31
  19.8 23.5 %collective-permute-done.1 = f32[1024,256]{1,0:T(8,128)S(1)} collective-permute-done((f32[1024,256]{1,0:T(8,128)S(1)}, f32[1024,256]{1,0:T(8,128)S(1)}, u32[]{:S(2)}, u32[]{:S(2)}) %collective-permute-start.1) | collective-permute-done | bytes 1048608 | tf_op jit(solution)/shard_map/ppermute | solution.py:31
  43.3 1.1 add.45
  44.4 2.8 collective-permute-start.2
  47.2 1.1 convert_element_type.7
  48.3 0.9 convert_element_type.6
  49.2 43.5 %collective-permute-done.2 = f32[1024,256]{1,0:T(8,128)} collective-permute-done((f32[1024,256]{1,0:T(8,128)}, f32[1024,256]{1,0:T(8,128)}, u32[]{:S(2)}, u32[]{:S(2)}) %collective-permute-start.2) | collective-permute-done | bytes 1048608 | tf_op jit(solution)/shard_map/ppermute | solution.py:31
  92.8 1.7 fusion.7
  94.5 194.6 %while.16 = (s32[]{:T(128)}, f32[128,256]{1,0:T(8,128)}, f32[128,256]{1,0:T(8,128)S(1)}, s32[]{:T(128)}, f32[128,256]{1,0:T(8,128)}, /*index=5*/f32[256,256]{1,0...) while((s32[]{:T(128)}, f32[128,256]{1,0:T(8,128)}, ...), condition=%wide.region_2.3_spmd.clone, body=%wide.region_0.2_spmd.clone.sunk | while | flops 201588736 | bytes 2490639 | solution.py:49
  94.5 2.0 convolution_select_fusion.2
  96.4 0.0 all-reduce.2.cloned.1.call-update
  96.5 44.7 %all-reduce.2.cloned.1.call-done = f32[128,256]{1,0:T(8,128)} async-done(((f32[128,256]{1,0:T(8,128)}), f32[128,256]{1,0:T(8,128)}) %all-reduce.2.cloned.1.call-update) | async-done | bytes 131088 | tf_op jit(solution)/shard_map/while/body/eval_jaxpr/psum | solution.py:9
  141.2 1.4 convolution_add_fusion.2
  142.6 1.6 select_select_fusion.2
  144.2 2.0 convolution_select_fusion.2
  146.1 0.0 all-reduce.2.cloned.1.call-update
  146.2 42.9 %all-reduce.2.cloned.1.call-done = f32[128,256]{1,0:T(8,128)} async-done(((f32[128,256]{1,0:T(8,128)}), f32[128,256]{1,0:T(8,128)}) %all-reduce.2.cloned.1.call-update) | async-done | bytes 131088 | tf_op jit(solution)/shard_map/while/body/eval_jaxpr/psum | solution.py:9
  189.0 1.4 convolution_add_fusion.2
  190.4 1.6 select_select_fusion.2
  192.0 2.0 convolution_select_fusion.2
  194.0 43.8 %all-reduce.2.cloned.1.call-done = f32[128,256]{1,0:T(8,128)} async-done(((f32[128,256]{1,0:T(8,128)}), f32[128,256]{1,0:T(8,128)}) %all-reduce.2.cloned.1.call-update) | async-done | bytes 131088 | tf_op jit(solution)/shard_map/while/body/eval_jaxpr/psum | solution.py:9
  237.8 1.4 convolution_add_fusion.2
  239.1 1.6 select_select_fusion.2
  240.7 2.0 convolution_select_fusion.2
  242.7 43.4 %all-reduce.2.cloned.1.call-done = f32[128,256]{1,0:T(8,128)} async-done(((f32[128,256]{1,0:T(8,128)}), f32[128,256]{1,0:T(8,128)}) %all-reduce.2.cloned.1.call-update) | async-done | bytes 131088 | tf_op jit(solution)/shard_map/while/body/eval_jaxpr/psum | solution.py:9
  286.2 1.4 convolution_add_fusion.2
  287.5 1.6 select_select_fusion.2
  (9 shorter events, 0.0 us)
Async XLA Ops:
  6.5 1.6 copy-start
  13.9 2.8 collective-permute-start
  16.8 26.5 %collective-permute-start.1 = (f32[1024,256]{1,0:T(8,128)S(1)}, f32[1024,256]{1,0:T(8,128)S(1)}, u32[]{:S(2)}, u32[]{:S(2)}) collective-permute-start(f32[1024,256]{1,0:T(8,128)S(1)} %add.44), channel_id=1, source_target_pairs={{0,2},{1,3},{2,0},{3,1},{4,6},{5,7},{6,4},{7,5},{8,10},{9,11},{10,... | collective-permute-start | bytes 3145736 | tf_op jit(solution)/shard_map/ppermute | solution.py:31
  44.4 48.4 %collective-permute-start.2 = (f32[1024,256]{1,0:T(8,128)}, f32[1024,256]{1,0:T(8,128)}, u32[]{:S(2)}, u32[]{:S(2)}) collective-permute-start(f32[1024,256]{1,0:T(8,128)} %add.45), channel_id=1, source_target_pairs={{0,4},{1,5},{2,6},{3,7},{4,0},{5,1},{6,2},{7,3},{8,12},{9,13},{10,... | collective-permute-start | bytes 3145736 | tf_op jit(solution)/shard_map/ppermute | solution.py:31
  94.5 46.7 %all-reduce.2.cloned.1.call-start = ((), (), s32[]{:S(2)}) async-start(), calls=%async_computation | async-start | bytes 262144 | tf_op jit(solution)/shard_map/while/body/eval_jaxpr/psum | solution.py:9
  144.2 44.9 %all-reduce.2.cloned.1.call-start = ((), (), s32[]{:S(2)}) async-start(), calls=%async_computation | async-start | bytes 262144 | tf_op jit(solution)/shard_map/while/body/eval_jaxpr/psum | solution.py:9
  192.0 45.8 %all-reduce.2.cloned.1.call-start = ((), (), s32[]{:S(2)}) async-start(), calls=%async_computation | async-start | bytes 262144 | tf_op jit(solution)/shard_map/while/body/eval_jaxpr/psum | solution.py:9
  240.7 45.4 %all-reduce.2.cloned.1.call-start = ((), (), s32[]{:S(2)}) async-start(), calls=%async_computation | async-start | bytes 262144 | tf_op jit(solution)/shard_map/while/body/eval_jaxpr/psum | solution.py:9
Sparse Core Ops, SparseCore 0:
  98.2 42.9 all-reduce.1
  147.9 41.1 all-reduce.1
  195.7 42.0 all-reduce.1
  244.1 41.9 all-reduce.1
